TPU v7x, 512 devices: a whole 4x4x16 slice. The times are simulated.
512 devices in a mesh: pairs: 64 (over y, z), days: 8 (over x, core).
Axes of the slice: x: 4, y: 4, z: 16, core: 2. Of those that a mesh axis runs over, the one named last changes fastest.
Arguments:
- spectra: bfloat16 [2, 64, 96, 30, 8, 256], P(None, 'pairs', 'days'), may hold values from -5 to 5
- held_block: int32 [64], replicated, may hold values from 0 to 63, as said below
- partner: int32 [64], replicated, may hold values from 0 to 63, as said below
Outputs:
- stacked: float32 [64, 8, 2, 256, 256], P('pairs', 'days')
Inputs may be any that keep to these rules, and one draw needn't show every extreme that they name: held_block is a permutation of the block numbers. partner[p] is the block held by device p - 1 or by device p + 1; devices 0 and 1 take each other, and so do devices 64 - 2 and 63.
All inputs are finite; a program needn't handle non-finite values.
Results may differ from a plain program's by a relative error of at most 0.0003.
Values may be sent and summed in bfloat16 or wider, within the bound.
A program may use at most 64 MiB of HBM per device.

v0:
```python
import math

import jax
import jax.numpy as jnp
from jax import lax
from jax.sharding import PartitionSpec as P


def with_halo(x, sides, width):
    for axis, dim in sides:
        count, length = (lax.axis_size(axis), x.shape[dim])
        up = [(i, (i + 1) % count) for i in range(count - 1)]
        down = [(j, i) for i, j in up]
        last = lax.slice_in_dim(x, length - width, length, axis=dim)
        leading = lax.slice_in_dim(x, 0, width, axis=dim)
        before = lax.ppermute(last, axis, up)
        after = lax.ppermute(leading, axis, down)
        x = jnp.concatenate([before, x, after], axis=dim)
    return x


def neighbours(block):
    return with_halo(block, (("pairs", 1),), 1)


def tile_product(own_rows, far_rows):
    real_part = jnp.einsum(
        "tfa,tfb->fab", own_rows[0], far_rows[0], preferred_element_type=jnp.float32
    )
    real_part = real_part + jnp.einsum(
        "tfa,tfb->fab", own_rows[1], far_rows[1], preferred_element_type=jnp.float32
    )
    imag_part = jnp.einsum(
        "tfa,tfb->fab", own_rows[1], far_rows[0], preferred_element_type=jnp.float32
    )
    imag_part = imag_part - jnp.einsum(
        "tfa,tfb->fab", own_rows[0], far_rows[1], preferred_element_type=jnp.float32
    )
    return jnp.stack([real_part, imag_part], 1)


def flatten_days(block):
    return block.reshape(2, block.shape[1] * block.shape[2], block.shape[3], block.shape[4])


def per_device(spectra, held_block, partner):
    position = lax.axis_index("pairs")
    positions = jnp.arange(held_block.shape[0], dtype=jnp.int32)
    wanted = jnp.sum(jnp.where(positions == position, partner, 0))
    holder = jnp.sum(jnp.where(held_block == wanted, positions, 0))
    side_index = holder - position + 1
    stacked_count = lax.axis_size("days") * spectra.shape[2] * spectra.shape[3]
    weighting = 1.0 / math.sqrt(stacked_count)
    padded = neighbours(spectra)
    far_block = lax.dynamic_index_in_dim(padded, side_index, 1, keepdims=False)
    own_flat = flatten_days(spectra[:, 0])
    far_flat = flatten_days(far_block)
    partials = lax.psum_scatter(
        tile_product(own_flat, far_flat), "days", scatter_dimension=0, tiled=True
    )
    return (partials * weighting)[None]


def solution(mesh):
    in_specs = (P(None, "pairs", "days", None, None, None), P(), P())
    out_specs = P("pairs", "days", None, None, None)
    return jax.shard_map(
        per_device, mesh=mesh, in_specs=in_specs, out_specs=out_specs, check_vma=False
    )
```

profile of v0, /device:TPU:24, one launch (start us, length us, event | category | flops | bytes accessed | tf_op | source)
XLA Modules:
  0.0 189.7 jit_solution(10977886706727287873)
XLA Ops:
  6.5 0.0 all-reduce.3.cloned.1.call-start
  6.5 3.8 %collective-permute-start = (bf16[2,1,12,30,8,256]{5,4,3,2,1,0:T(8,128)(2,1)}, bf16[2,1,12,30,8,256]{5,4,3,2,1,0:T(8,128)(2,1)S(1)}, u32[]{:S(2)}, u32[]{:S(2)}) collective-permute-start(bf16[2,1,12,30,8,256]{5,4,3,2,1,0:T(8,128)(2,1)} %param.3), channel_id=1, source_target_pairs={{0,8},{8,16},{16,24},{24,32},{32,40},{40,48},{48,56},{56,64},{64,7... | collective-permute-start | bytes 8847368 | tf_op jit(solution)/shard_map/ppermute | solution.py:16
  10.4 9.7 %collective-permute-start.1 = (bf16[2,1,12,30,8,256]{5,4,3,2,1,0:T(8,128)(2,1)}, bf16[2,1,12,30,8,256]{5,4,3,2,1,0:T(8,128)(2,1)}, u32[]{:S(2)}, u32[]{:S(2)}) collective-permute-start(bf16[2,1,12,30,8,256]{5,4,3,2,1,0:T(8,128)(2,1)} %param.3), channel_id=1, source_target_pairs={{8,0},{16,8},{24,16},{32,24},{40,32},{48,40},{56,48},{64,56},{72,6... | collective-permute-start | bytes 8847368 | tf_op jit(solution)/shard_map/ppermute | solution.py:17
  20.1 1.3 fusion.13
  21.3 1.9 %fusion.14 = s32[]{:T(128)} fusion(s32[64]{0:T(128)} %param.4, s32[]{:T(128)} %fusion.13), kind=kLoop, calls=%fused_computation.23 | loop fusion | flops 191 | bytes 264 | tf_op jit(solution)/shard_map/reduce_sum | solution.py:50
  23.9 0.0 copy-start
  23.9 2.2 %fusion.16 = (bf16[1,1,12,30,8,256]{5,4,3,2,1,0:T(8,128)(2,1)S(1)}, bf16[1,1,12,30,8,256]{5,4,3,2,1,0:T(8,128)(2,1)S(1)}) fusion(bf16[2,1,12,30,8,256]{5,4,3,2,1,0:T(8,128)(2,1)} %param.3), kind=kLoop, calls=%fused_computation.25 | loop fusion | bytes 5898240 | tf_op jit(solution)/shard_map/slice | solution.py:31
  26.0 56.2 %collective-permute-done = bf16[2,1,12,30,8,256]{5,4,3,2,1,0:T(8,128)(2,1)S(1)} collective-permute-done((bf16[2,1,12,30,8,256]{5,4,3,2,1,0:T(8,128)(2,1)}, bf16[2,1,12,30,8,256]{5,4,3,2,1,0:T(8,128)(2,1)S(1)}, u32[]{:S(2)}, u32[]{:S(2)}) %collective-permute-start) | collective-permute-done | bytes 2949152 | tf_op jit(solution)/shard_map/ppermute | solution.py:16
  82.2 1.3 collective-permute-done.1
  83.5 0.0 copy-done
  83.5 1.7 fusion.1
  85.2 0.2 fusion.15
  85.4 1.1 fusion.3
  86.5 1.1 fusion.5
  87.6 1.1 add_bitcast_fusion
  88.7 1.1 subtract_bitcast_fusion
  89.8 2.2 %pad_maximum_fusion = f32[8,2,256,256]{2,3,0,1:T(8,128)} fusion(f32[8,1,256,256]{2,3,0,1:T(8,128)S(1)} %subtract_bitcast_fusion, f32[8,1,256,256]{2,3,0,1:T(8,128)S(1)} %add_bitcast_fusion), kind=kLoop, calls=%fused_computation.3 | loop fusion | flops 1048576 | bytes 8388608 | tf_op jit(solution)/shard_map/stack | solution.py:39
  92.1 0.0 all-reduce.3.cloned.1.call-update
  92.1 1.3 dynamic-slice
  93.4 86.8 %all-reduce.3.cloned.1.call-done = f32[8,2,256,256]{2,3,0,1:T(8,128)} async-done(((f32[8,2,256,256]{2,3,0,1:T(8,128)}), f32[8,2,256,256]{2,3,0,1:T(8,128)}) %all-reduce.3.cloned.1.call-update) | async-done | bytes 4194320
  180.1 1.7 fusion.12
  181.9 1.0 copy.26
Async XLA Ops:
  6.5 173.6 %all-reduce.3.cloned.1.call-start = ((), (), s32[]{:S(2)}) async-start(), calls=%async_computation | async-start | bytes 8388608
  6.5 75.7 %collective-permute-start = (bf16[2,1,12,30,8,256]{5,4,3,2,1,0:T(8,128)(2,1)}, bf16[2,1,12,30,8,256]{5,4,3,2,1,0:T(8,128)(2,1)S(1)}, u32[]{:S(2)}, u32[]{:S(2)}) collective-permute-start(bf16[2,1,12,30,8,256]{5,4,3,2,1,0:T(8,128)(2,1)} %param.3), channel_id=1, source_target_pairs={{0,8},{8,16},{16,24},{24,32},{32,40},{40,48},{48,56},{56,64},{64,7... | collective-permute-start | bytes 8847368 | tf_op jit(solution)/shard_map/ppermute | solution.py:16
  10.4 73.1 %collective-permute-start.1 = (bf16[2,1,12,30,8,256]{5,4,3,2,1,0:T(8,128)(2,1)}, bf16[2,1,12,30,8,256]{5,4,3,2,1,0:T(8,128)(2,1)}, u32[]{:S(2)}, u32[]{:S(2)}) collective-permute-start(bf16[2,1,12,30,8,256]{5,4,3,2,1,0:T(8,128)(2,1)} %param.3), channel_id=1, source_target_pairs={{8,0},{16,8},{24,16},{32,24},{40,32},{48,40},{56,48},{64,56},{72,6... | collective-permute-start | bytes 8847368 | tf_op jit(solution)/shard_map/ppermute | solution.py:17
  23.9 59.6 %copy-start = (bf16[2,1,12,30,8,256]{5,4,3,2,1,0:T(8,128)(2,1)S(1)}, bf16[2,1,12,30,8,256]{5,4,3,2,1,0:T(8,128)(2,1)}, u32[]{:S(2)}) copy-start(bf16[2,1,12,30,8,256]{5,4,3,2,1,0:T(8,128)(2,1)} %param.3) | copy-start | bytes 8847364
Sparse Core Ops, SparseCore 0:
  92.2 87.8 all-reduce.2
where the time goes:
time: 190 us
  waiting for transfers between devices  144 us (76%)
  between operations  14.1 us (7%)
  starting transfers between devices  13.5 us (7%)
  other arithmetic  8.86 us (5%)
  local copies, waits for them, and re-layouts  4.62 us (2%)
  matrix products  4.44 us (2%)
    unnamed x2, waiting for transfers between devices  86.8 us
    ppermute x1, waiting for transfers between devices, with_halo(): before = lax.ppermute(last, axis, up)  56.2 us
    ppermute x1, starting transfers between devices, with_halo(): after = lax.ppermute(leading, axis, down)  9.68 us
    ppermute x1, starting transfers between devices, with_halo(): before = lax.ppermute(last, axis, up)  3.82 us
  transfers between devices with their start and end apart: 3, of which 3 were waited for; matrix products, arithmetic and copies ran while one was open for 4% of the time, Pallas kernels for 0%

commit v1 on v0

v1 whole, which is shorter than its diff:
```python
import functools
import math

import jax
import jax.numpy as jnp
from jax import lax
from jax.experimental import pallas as pl
from jax.experimental.pallas import tpu as pltpu
from jax.sharding import PartitionSpec as P

MESH = pl.DeviceIdType.MESH
LANES = 128
GROUP = 8
STEP = 24


def kernel(
    n_pairs, n_x, weight, held_ref, partner_ref, x_ref, out_ref,
    x_in, stage, grid_own, to_core, far, wide, tiles, parts, back, view,
    in_sem, core_send, core_recv, z_send, z_recv, part_send, part_recv, back_send, back_recv,
):
    n_time = x_in.shape[1]
    n_tiles = 2 * n_x
    p = lax.axis_index("pairs")
    d = lax.axis_index("days")
    x = d // 2
    core = d % 2
    up = 1 - 2 * core
    z_to = (p + up + n_pairs) % n_pairs
    z_from = (p - up + n_pairs) % n_pairs
    other = d + 1 - 2 * core

    barrier = pltpu.get_barrier_semaphore()
    peers = [(p, other), (z_to, d), (z_from, d)]
    peers += [(p, (x + k) % n_x * 2 + core) for k in range(1, n_x)]
    for peer in peers:
        pl.semaphore_signal(barrier, inc=1, device_id=peer, device_id_type=MESH)

    chunks = in_sem.shape[0]
    rows = n_time // chunks
    loads = [
        pltpu.make_async_copy(
            x_ref.at[:, pl.ds(k * rows, rows)], x_in.at[:, pl.ds(k * rows, rows)], in_sem.at[k]
        )
        for k in range(chunks)
    ]
    for load in loads:
        load.start()

    bins = 2 * n_x

    def relayout(i, carry):
        t0 = pl.multiple_of(i * STEP, GROUP)
        for part in range(2):
            block = x_in[part, pl.ds(t0, STEP)].astype(jnp.float32).reshape(STEP * bins, 2 * LANES)
            stage[part, 0] = block[:, :LANES]
            stage[part, 1] = block[:, LANES:]
        r0 = pl.multiple_of(i * 2 * STEP, 16)
        for f in range(bins):
            for half in range(2):
                both = [
                    stage[part, half, pl.ds(f, STEP, stride=bins), :].reshape(STEP // GROUP, 1, GROUP, LANES)
                    for part in range(2)
                ]
                block = jnp.concatenate(both, axis=1).reshape(2 * STEP, LANES).astype(jnp.bfloat16)
                where = (f + core) % 2 * n_x + f // 2
                grid_own[where, half, pl.ds(r0, 2 * STEP), :] = block
        return carry

    for k in range(chunks):
        loads[k].wait()
        lax.fori_loop(k * (rows // STEP), (k + 1) * (rows // STEP), relayout, 0)

    pl.semaphore_wait(barrier, len(peers))

    def owner(i):
        return (x + 1 + i) % n_x

    def core_copy(i):
        return pltpu.make_async_remote_copy(
            src_ref=grid_own.at[n_x + owner(i)],
            dst_ref=to_core.at[owner(i)],
            send_sem=core_send.at[i],
            recv_sem=core_recv.at[i],
            device_id=(p, other),
            device_id_type=MESH,
        )

    def z_copy(q, source):
        held = grid_own if source == 0 else to_core
        return pltpu.make_async_remote_copy(
            src_ref=held.at[owner(q // 2), q % 2],
            dst_ref=far.at[q, source],
            send_sem=z_send.at[q, source],
            recv_sem=z_recv.at[q, source],
            device_id=(z_to, d),
            device_id_type=MESH,
        )

    def part_copy(q):
        return pltpu.make_async_remote_copy(
            src_ref=tiles.at[q],
            dst_ref=parts.at[q],
            send_sem=part_send.at[q],
            recv_sem=part_recv.at[q],
            device_id=(p, owner(q // 2) * 2 + core),
            device_id_type=MESH,
        )

    def back_copy(half):
        return pltpu.make_async_remote_copy(
            src_ref=tiles.at[n_tiles - 2 + half],
            dst_ref=back.at[half],
            send_sem=back_send.at[half],
            recv_sem=back_recv.at[half],
            device_id=(z_from, d),
            device_id_type=MESH,
        )

    z_copy(0, 0).start()
    for i in range(n_x):
        core_copy(i).start()
    core_copy(0).wait_recv()
    z_copy(0, 1).start()

    def one_tile(q, carry):
        i, half = q // 2, q % 2

        @pl.when((half == 1) & (i < n_x - 1))
        def _():
            core_copy(i + 1).wait_recv()

        @pl.when(q < n_tiles - 1)
        def _():
            z_copy(q + 1, 0).start()
            z_copy(q + 1, 1).start()

        for source, held in enumerate((grid_own, to_core)):
            for side in range(2):
                own = held[owner(i), side]
                wide[:, pl.ds(side * LANES, LANES)] = own
                own = own.astype(jnp.float32).reshape(-1, 2, GROUP, LANES)
                turned = jnp.concatenate([-own[:, 1:], own[:, :1]], axis=1)
                wide[:, pl.ds((2 + side) * LANES, LANES)] = turned.reshape(-1, LANES).astype(jnp.bfloat16)
            z_copy(q, source).wait_recv()
            product = lax.dot_general(
                far[q, source], wide[...], (((0,), (0,)), ((), ())), preferred_element_type=jnp.float32
            )
            if source == 0:
                tiles[q] = product
            else:
                tiles[q] += product

        @pl.when(i < n_x - 1)
        def _():
            part_copy(q).start()

        @pl.when(i == n_x - 1)
        def _():
            for k in range(n_x - 1):
                part_copy(2 * k + half).wait_recv()
                tiles[q] += parts[2 * k + half]
            back_copy(half).start()

        return carry

    lax.fori_loop(0, n_tiles, one_tile, 0)

    for half in range(2):
        tile = tiles[n_tiles - 2 + half]
        view[0, :, pl.ds(half * LANES, LANES)] = tile[:, : 2 * LANES].T
        view[1, :, pl.ds(half * LANES, LANES)] = -tile[:, 2 * LANES :].T
    mine = held_ref[z_from] == partner_ref[p]
    for half in range(2):
        back_copy(half).wait_recv()
        spot = pl.ds(half * LANES, LANES)
        for part in range(2):
            sent = back[half, :, pl.ds(part * 2 * LANES, 2 * LANES)]
            out_ref[part, spot, :] = jnp.where(mine, view[part, spot, :], sent) * weight

    for i in range(n_x):
        core_copy(i).wait_send()
    for q in range(n_tiles):
        z_copy(q, 0).wait_send()
        z_copy(q, 1).wait_send()
    for q in range(n_tiles - 2):
        part_copy(q).wait_send()
    for half in range(2):
        back_copy(half).wait_send()


def per_device(spectra, held_block, partner):
    n_pairs, n_days = lax.axis_size("pairs"), lax.axis_size("days")
    _, _, days, segments, bins, channels = spectra.shape
    n_time = days * segments
    n_x, n_tiles = n_days // 2, n_days
    block = 2 * n_time
    weight = 1.0 / math.sqrt(n_days * n_time)
    dma = pltpu.SemaphoreType.DMA
    out = pl.pallas_call(
        functools.partial(kernel, n_pairs, n_x, weight),
        out_shape=jax.ShapeDtypeStruct((2, channels, channels), jnp.float32),
        in_specs=[
            pl.BlockSpec(memory_space=pltpu.SMEM),
            pl.BlockSpec(memory_space=pltpu.SMEM),
            pl.BlockSpec(memory_space=pl.ANY),
        ],
        out_specs=pl.BlockSpec(memory_space=pltpu.VMEM),
        scratch_shapes=[
            pltpu.VMEM((2, n_time, bins, channels), jnp.bfloat16),
            pltpu.VMEM((2, 2, STEP * bins, LANES), jnp.float32),
            pltpu.VMEM((bins, 2, block, LANES), jnp.bfloat16),
            pltpu.VMEM((n_x, 2, block, LANES), jnp.bfloat16),
            pltpu.VMEM((n_tiles, 2, block, LANES), jnp.bfloat16),
            pltpu.VMEM((block, 4 * LANES), jnp.bfloat16),
            pltpu.VMEM((n_tiles, LANES, 4 * LANES), jnp.float32),
            pltpu.VMEM((n_tiles - 2, LANES, 4 * LANES), jnp.float32),
            pltpu.VMEM((2, LANES, 4 * LANES), jnp.float32),
            pltpu.VMEM((2, channels, channels), jnp.float32),
            dma((3,)),
            dma((n_x,)),
            dma((n_x,)),
            dma((n_tiles, 2)),
            dma((n_tiles, 2)),
            dma((n_tiles - 2,)),
            dma((n_tiles - 2,)),
            dma((2,)),
            dma((2,)),
        ],
        compiler_params=pltpu.CompilerParams(
            collective_id=0, has_side_effects=True, vmem_limit_bytes=48 * 1024 * 1024
        ),
        cost_estimate=pl.CostEstimate(flops=8 * bins * n_time * channels**2, bytes_accessed=4 * block * bins * channels, transcendentals=0),
    )(held_block, partner, spectra.reshape(2, n_time, bins, channels))
    return out[None, None]


def solution(mesh):
    in_specs = (P(None, "pairs", "days", None, None, None), P(), P())
    out_specs = P("pairs", "days", None, None, None)
    return jax.shard_map(
        per_device, mesh=mesh, in_specs=in_specs, out_specs=out_specs, check_vma=False
    )
```

time: 190 us -> 64.9 us (0.34)
  the two profiles are of different devices: /device:TPU:24 before, /device:TPU:1 now
where the time goes in v1:
time: 64.9 us; the launch traced here: 64.7 us
  Pallas kernels  60.7 us (94%)
  local copies, waits for them, and re-layouts  3.94 us (6%)
    pallas_call x1, Pallas kernels, per_device(): pl.pallas_call(functools.partial(kernel, n_pairs, n_x, weight), out_shape...  60.7 us
    unnamed x7, local copies, waits for them, and re-layouts  3.94 us

profile of v1, /device:TPU:1, one launch (start us, length us, event | category | flops | bytes accessed | tf_op | source)
XLA Modules:
  0.0 64.7 jit_solution(7438887347175122243)
XLA Ops:
  0.0 0.0 copy-start
  0.0 1.8 %copy-done = bf16[2,1,12,30,8,256]{5,4,3,2,1,0:T(8,128)(2,1)S(1)} copy-done((bf16[2,1,12,30,8,256]{5,4,3,2,1,0:T(8,128)(2,1)S(1)}, bf16[2,1,12,30,8,256]{5,4,3,2,1,0:T(8,128)(2,1)}, u32[]{:S(2)}) %copy-start) | copy-done | bytes 2949144
  1.8 0.0 copy-start.1
  1.8 0.7 %copy-done.1 = s32[64]{0:T(128)S(1)} copy-done((s32[64]{0:T(128)S(1)}, s32[64]{0:T(128)}, u32[]{:S(2)}) %copy-start.1) | copy-done | bytes 280
  2.5 0.0 copy-start.2
  2.5 0.7 %copy-done.2 = s32[64]{0:T(128)S(1)} copy-done((s32[64]{0:T(128)S(1)}, s32[64]{0:T(128)}, u32[]{:S(2)}) %copy-start.2) | copy-done | bytes 280
  3.1 60.7 %shard_map.37 = f32[2,256,256]{2,1,0:T(8,128)S(1)} custom-call(s32[64]{0:T(128)S(1)} %copy-done.1, s32[64]{0:T(128)S(1)} %copy-done.2, bf16[2,360,8,256]{3,2,1,0:T(8,128)(2,1)S(1)} %bitcast.3), custom_call_target="tpu_custom_call" | custom-call | flops 1509949440 | bytes 5898240 | tf_op jit(solution)/shard_map/pallas_call | solution.py:200
  63.9 0.8 %copy.5 = f32[1,1,2,256,256]{4,3,2,1,0:T(8,128)} copy(f32[1,1,2,256,256]{4,3,2,1,0:T(8,128)S(1)} %bitcast.2) | data formatting | bytes 1048576
Async XLA Ops:
  0.0 1.8 %copy-start = (bf16[2,1,12,30,8,256]{5,4,3,2,1,0:T(8,128)(2,1)S(1)}, bf16[2,1,12,30,8,256]{5,4,3,2,1,0:T(8,128)(2,1)}, u32[]{:S(2)}) copy-start(bf16[2,1,12,30,8,256]{5,4,3,2,1,0:T(8,128)(2,1)} %param.3) | copy-start | bytes 8847364
  1.8 0.7 %copy-start.1 = (s32[64]{0:T(128)S(1)}, s32[64]{0:T(128)}, u32[]{:S(2)}) copy-start(s32[64]{0:T(128)} %held_ref.1) | copy-start | bytes 772
  2.5 0.7 %copy-start.2 = (s32[64]{0:T(128)S(1)}, s32[64]{0:T(128)}, u32[]{:S(2)}) copy-start(s32[64]{0:T(128)} %partner_ref.1) | copy-start | bytes 772

commit v2 on v1

--- a/solution.py
+++ b/solution.py
@@ -15,8 +15,8 @@
 
 
 def kernel(
-    n_pairs, n_x, weight, held_ref, partner_ref, x_ref, out_ref,
-    x_in, stage, grid_own, to_core, far, wide, tiles, parts, back, view,
+    n_pairs, n_x, weight, held_hbm, partner_hbm, x_ref, out_ref,
+    held_ref, partner_ref,    x_in, stage, grid_own, to_core, far, wide, tiles, parts, back, view,
     in_sem, core_send, core_recv, z_send, z_recv, part_send, part_recv, back_send, back_recv,
 ):
     n_time = x_in.shape[1]
@@ -29,14 +29,20 @@
     z_to = (p + up + n_pairs) % n_pairs
     z_from = (p - up + n_pairs) % n_pairs
     other = d + 1 - 2 * core
+    last = (n_pairs - 1) * core
+    has_from = p != last
+    has_to = p != n_pairs - 1 - last
 
     barrier = pltpu.get_barrier_semaphore()
-    peers = [(p, other), (z_to, d), (z_from, d)]
-    peers += [(p, (x + k) % n_x * 2 + core) for k in range(1, n_x)]
+    peers = [(p, other)] + [(p, (x + k) % n_x * 2 + core) for k in range(1, n_x)]
     for peer in peers:
         pl.semaphore_signal(barrier, inc=1, device_id=peer, device_id_type=MESH)
 
-    chunks = in_sem.shape[0]
+    @pl.when(has_from)
+    def _():
+        pl.semaphore_signal(barrier, inc=1, device_id=(z_from, d), device_id_type=MESH)
+
+    chunks = in_sem.shape[0] - 2
     rows = n_time // chunks
     loads = [
         pltpu.make_async_copy(
@@ -44,7 +50,11 @@
         )
         for k in range(chunks)
     ]
-    for load in loads:
+    orders = [
+        pltpu.make_async_copy(held_hbm, held_ref, in_sem.at[chunks]),
+        pltpu.make_async_copy(partner_hbm, partner_ref, in_sem.at[chunks + 1]),
+    ]
+    for load in loads + orders:
         load.start()
 
     bins = 2 * n_x
@@ -71,7 +81,7 @@
         loads[k].wait()
         lax.fori_loop(k * (rows // STEP), (k + 1) * (rows // STEP), relayout, 0)
 
-    pl.semaphore_wait(barrier, len(peers))
+    pl.semaphore_wait(barrier, len(peers) + has_to.astype(jnp.int32))
 
     def owner(i):
         return (x + 1 + i) % n_x
@@ -117,23 +127,25 @@
             device_id_type=MESH,
         )
 
-    z_copy(0, 0).start()
+    @pl.when(has_to)
+    def _():
+        z_copy(0, 0).start()
+
     for i in range(n_x):
         core_copy(i).start()
-    core_copy(0).wait_recv()
-    z_copy(0, 1).start()
+    for i in range(n_x):
+        core_copy(i).wait_recv()
+
+        @pl.when(has_to)
+        def _():
+            if i > 0:
+                z_copy(2 * i, 0).start()
+            z_copy(2 * i, 1).start()
+            z_copy(2 * i + 1, 0).start()
+            z_copy(2 * i + 1, 1).start()
 
     def one_tile(q, carry):
         i, half = q // 2, q % 2
-
-        @pl.when((half == 1) & (i < n_x - 1))
-        def _():
-            core_copy(i + 1).wait_recv()
-
-        @pl.when(q < n_tiles - 1)
-        def _():
-            z_copy(q + 1, 0).start()
-            z_copy(q + 1, 1).start()
 
         for source, held in enumerate((grid_own, to_core)):
             for side in range(2):
@@ -164,15 +176,31 @@
 
         return carry
 
-    lax.fori_loop(0, n_tiles, one_tile, 0)
-
-    for half in range(2):
-        tile = tiles[n_tiles - 2 + half]
-        view[0, :, pl.ds(half * LANES, LANES)] = tile[:, : 2 * LANES].T
-        view[1, :, pl.ds(half * LANES, LANES)] = -tile[:, 2 * LANES :].T
+    @pl.when(has_from)
+    def _():
+        lax.fori_loop(0, n_tiles, one_tile, 0)
+        for half in range(2):
+            tile = tiles[n_tiles - 2 + half]
+            view[0, :, pl.ds(half * LANES, LANES)] = tile[:, : 2 * LANES].T
+            view[1, :, pl.ds(half * LANES, LANES)] = -tile[:, 2 * LANES :].T
+
+    @pl.when(jnp.logical_not(has_from))
+    def _():
+        view[...] = jnp.zeros_like(view)
+
+    @pl.when(jnp.logical_not(has_to))
+    def _():
+        back[...] = jnp.zeros_like(back)
+
+    for order in orders:
+        order.wait()
     mine = held_ref[z_from] == partner_ref[p]
     for half in range(2):
-        back_copy(half).wait_recv()
+
+        @pl.when(has_to)
+        def _():
+            back_copy(half).wait_recv()
+
         spot = pl.ds(half * LANES, LANES)
         for part in range(2):
             sent = back[half, :, pl.ds(part * 2 * LANES, 2 * LANES)]
@@ -180,13 +208,19 @@
 
     for i in range(n_x):
         core_copy(i).wait_send()
-    for q in range(n_tiles):
-        z_copy(q, 0).wait_send()
-        z_copy(q, 1).wait_send()
-    for q in range(n_tiles - 2):
-        part_copy(q).wait_send()
-    for half in range(2):
-        back_copy(half).wait_send()
+
+    @pl.when(has_to)
+    def _():
+        for q in range(n_tiles):
+            z_copy(q, 0).wait_send()
+            z_copy(q, 1).wait_send()
+
+    @pl.when(has_from)
+    def _():
+        for q in range(n_tiles - 2):
+            part_copy(q).wait_send()
+        for half in range(2):
+            back_copy(half).wait_send()
 
 
 def per_device(spectra, held_block, partner):
@@ -201,12 +235,14 @@
         functools.partial(kernel, n_pairs, n_x, weight),
         out_shape=jax.ShapeDtypeStruct((2, channels, channels), jnp.float32),
         in_specs=[
-            pl.BlockSpec(memory_space=pltpu.SMEM),
-            pl.BlockSpec(memory_space=pltpu.SMEM),
-            pl.BlockSpec(memory_space=pl.ANY),
+            pl.BlockSpec(memory_space=pltpu.HBM),
+            pl.BlockSpec(memory_space=pltpu.HBM),
+            pl.BlockSpec(memory_space=pltpu.HBM),
         ],
         out_specs=pl.BlockSpec(memory_space=pltpu.VMEM),
         scratch_shapes=[
+            pltpu.SMEM((n_pairs,), jnp.int32),
+            pltpu.SMEM((n_pairs,), jnp.int32),
             pltpu.VMEM((2, n_time, bins, channels), jnp.bfloat16),
             pltpu.VMEM((2, 2, STEP * bins, LANES), jnp.float32),
             pltpu.VMEM((bins, 2, block, LANES), jnp.bfloat16),
@@ -217,7 +253,7 @@
             pltpu.VMEM((n_tiles - 2, LANES, 4 * LANES), jnp.float32),
             pltpu.VMEM((2, LANES, 4 * LANES), jnp.float32),
             pltpu.VMEM((2, channels, channels), jnp.float32),
-            dma((3,)),
+            dma((5,)),
             dma((n_x,)),
             dma((n_x,)),
             dma((n_tiles, 2)),
@@ -228,7 +264,7 @@
             dma((2,)),
         ],
         compiler_params=pltpu.CompilerParams(
-            collective_id=0, has_side_effects=True, vmem_limit_bytes=48 * 1024 * 1024
+            collective_id=0, has_side_effects=True, vmem_limit_bytes=62 * 1024 * 1024
         ),
         cost_estimate=pl.CostEstimate(flops=8 * bins * n_time * channels**2, bytes_accessed=4 * block * bins * channels, transcendentals=0),
     )(held_block, partner, spectra.reshape(2, n_time, bins, channels))

time: 64.9 us -> 59.5 us (0.917)
  the two profiles are of different devices: /device:TPU:1 before, /device:TPU:27 now
where the time goes in v2:
time: 59.5 us; the launch traced here: 59.3 us
  Pallas kernels  57.5 us (97%)
  local copies, waits for them, and re-layouts  1.87 us (3%)
    pallas_call x1, Pallas kernels, per_device(): pl.pallas_call(functools.partial(kernel, n_pairs, n_x, weight), out_shape...  57.5 us
    unnamed x1, local copies, waits for them, and re-layouts  1.87 us

profile of v2, /device:TPU:27, one launch (start us, length us, event | category | flops | bytes accessed | tf_op | source)
XLA Modules:
  0.0 59.3 jit_solution(15090783214183626297)
XLA Ops:
  0.0 57.5 %shard_map.37 = f32[2,256,256]{2,1,0:T(8,128)} custom-call(s32[64]{0:T(128)} %held_hbm.1, s32[64]{0:T(128)} %partner_hbm.1, bf16[2,360,8,256]{3,2,1,0:T(8,128)(2,1)} %bitcast.3), custom_call_target="tpu_custom_call" | custom-call | flops 1509949440 | bytes 5898240 | tf_op jit(solution)/shard_map/pallas_call | solution.py:234
  57.5 1.9 %copy.5 = f32[1,1,2,256,256]{4,3,2,1,0:T(8,128)} copy(f32[1,1,2,256,256]{4,3,2,1,0:T(8,128)} %bitcast.2) | data formatting | bytes 1048576

commit v3 on v2

--- a/solution.py
+++ b/solution.py
@@ -11,12 +11,14 @@
 MESH = pl.DeviceIdType.MESH
 LANES = 128
 GROUP = 8
+LEVELS = 32767.0
+TINY = 2e-34
 STEP = 24
 
 
 def kernel(
     n_pairs, n_x, weight, held_hbm, partner_hbm, x_ref, out_ref,
-    held_ref, partner_ref,    x_in, stage, grid_own, to_core, far, wide, tiles, parts, back, view,
+    held_ref, partner_ref,    x_in, stage, grid_own, to_core, far, wide, tiles, parts, sent, sent_top, back, back_top, view,
     in_sem, core_send, core_recv, z_send, z_recv, part_send, part_recv, back_send, back_recv,
 ):
     n_time = x_in.shape[1]
@@ -58,6 +60,10 @@
         load.start()
 
     bins = 2 * n_x
+
+    def owner(i):
+        return (x + up * (1 + i) + n_x) % n_x
+
 
     def relayout(i, carry):
         t0 = pl.multiple_of(i * STEP, GROUP)
@@ -77,19 +83,11 @@
                 grid_own[where, half, pl.ds(r0, 2 * STEP), :] = block
         return carry
 
-    for k in range(chunks):
-        loads[k].wait()
-        lax.fori_loop(k * (rows // STEP), (k + 1) * (rows // STEP), relayout, 0)
-
-    pl.semaphore_wait(barrier, len(peers) + has_to.astype(jnp.int32))
-
-    def owner(i):
-        return (x + 1 + i) % n_x
-
     def core_copy(i):
+        theirs = (x - up * (1 + i) + n_x) % n_x
         return pltpu.make_async_remote_copy(
-            src_ref=grid_own.at[n_x + owner(i)],
-            dst_ref=to_core.at[owner(i)],
+            src_ref=grid_own.at[n_x + theirs],
+            dst_ref=to_core.at[theirs],
             send_sem=core_send.at[i],
             recv_sem=core_recv.at[i],
             device_id=(p, other),
@@ -117,19 +115,37 @@
             device_id_type=MESH,
         )
 
-    def back_copy(half):
-        return pltpu.make_async_remote_copy(
-            src_ref=tiles.at[n_tiles - 2 + half],
-            dst_ref=back.at[half],
-            send_sem=back_send.at[half],
-            recv_sem=back_recv.at[half],
-            device_id=(z_from, d),
-            device_id_type=MESH,
-        )
-
-    @pl.when(has_to)
-    def _():
-        z_copy(0, 0).start()
+    def back_copies(half):
+        return [
+            pltpu.make_async_remote_copy(
+                src_ref=source.at[half],
+                dst_ref=target.at[half],
+                send_sem=back_send.at[half, k],
+                recv_sem=back_recv.at[half, k],
+                device_id=(z_from, d),
+                device_id_type=MESH,
+            )
+            for k, (source, target) in enumerate(((sent_top, back_top), (sent, back)))
+        ]
+
+    for k in range(chunks):
+        loads[k].wait()
+        lax.fori_loop(k * (rows // STEP), (k + 1) * (rows // STEP), relayout, 0)
+        if k == 0:
+            pl.semaphore_wait(barrier, len(peers) + has_to.astype(jnp.int32))
+
+        @pl.when(has_to)
+        def _():
+            for q in range(2):
+                part = pl.ds(k * 2 * rows, 2 * rows)
+                pltpu.make_async_remote_copy(
+                    src_ref=grid_own.at[owner(0), q, part],
+                    dst_ref=far.at[q, 0, part],
+                    send_sem=z_send.at[q, 0],
+                    recv_sem=z_recv.at[q, 0],
+                    device_id=(z_to, d),
+                    device_id_type=MESH,
+                ).start()
 
     for i in range(n_x):
         core_copy(i).start()
@@ -141,7 +157,8 @@
             if i > 0:
                 z_copy(2 * i, 0).start()
             z_copy(2 * i, 1).start()
-            z_copy(2 * i + 1, 0).start()
+            if i > 0:
+                z_copy(2 * i + 1, 0).start()
             z_copy(2 * i + 1, 1).start()
 
     def one_tile(q, carry):
@@ -172,7 +189,12 @@
             for k in range(n_x - 1):
                 part_copy(2 * k + half).wait_recv()
                 tiles[q] += parts[2 * k + half]
-            back_copy(half).start()
+            tile = tiles[q]
+            top = jnp.maximum(jnp.max(jnp.abs(tile), axis=0, keepdims=True), TINY)
+            sent_top[half] = jnp.broadcast_to(top, sent_top.shape[1:])
+            sent[half] = jnp.round(tile * (LEVELS / top)).astype(jnp.int32).astype(jnp.int16)
+            for copy in back_copies(half):
+                copy.start()
 
         return carry
 
@@ -191,6 +213,7 @@
     @pl.when(jnp.logical_not(has_to))
     def _():
         back[...] = jnp.zeros_like(back)
+        back_top[...] = jnp.zeros_like(back_top)
 
     for order in orders:
         order.wait()
@@ -199,12 +222,14 @@
 
         @pl.when(has_to)
         def _():
-            back_copy(half).wait_recv()
+            for copy in back_copies(half):
+                copy.wait_recv()
 
         spot = pl.ds(half * LANES, LANES)
         for part in range(2):
-            sent = back[half, :, pl.ds(part * 2 * LANES, 2 * LANES)]
-            out_ref[part, spot, :] = jnp.where(mine, view[part, spot, :], sent) * weight
+            lanes = pl.ds(part * 2 * LANES, 2 * LANES)
+            theirs = back[half, :, lanes].astype(jnp.int32).astype(jnp.float32) * (back_top[half, :1, lanes] / LEVELS)
+            out_ref[part, spot, :] = jnp.where(mine, view[part, spot, :], theirs) * weight
 
     for i in range(n_x):
         core_copy(i).wait_send()
@@ -220,7 +245,8 @@
         for q in range(n_tiles - 2):
             part_copy(q).wait_send()
         for half in range(2):
-            back_copy(half).wait_send()
+            for copy in back_copies(half):
+                copy.wait_send()
 
 
 def per_device(spectra, held_block, partner):
@@ -231,6 +257,7 @@
     block = 2 * n_time
     weight = 1.0 / math.sqrt(n_days * n_time)
     dma = pltpu.SemaphoreType.DMA
+    operands = (held_block, partner, spectra.reshape(2, n_time, bins, channels))
     out = pl.pallas_call(
         functools.partial(kernel, n_pairs, n_x, weight),
         out_shape=jax.ShapeDtypeStruct((2, channels, channels), jnp.float32),
@@ -251,7 +278,10 @@
             pltpu.VMEM((block, 4 * LANES), jnp.bfloat16),
             pltpu.VMEM((n_tiles, LANES, 4 * LANES), jnp.float32),
             pltpu.VMEM((n_tiles - 2, LANES, 4 * LANES), jnp.float32),
-            pltpu.VMEM((2, LANES, 4 * LANES), jnp.float32),
+            pltpu.VMEM((2, LANES, 4 * LANES), jnp.int16),
+            pltpu.VMEM((2, GROUP, 4 * LANES), jnp.float32),
+            pltpu.VMEM((2, LANES, 4 * LANES), jnp.int16),
+            pltpu.VMEM((2, GROUP, 4 * LANES), jnp.float32),
             pltpu.VMEM((2, channels, channels), jnp.float32),
             dma((5,)),
             dma((n_x,)),
@@ -260,14 +290,14 @@
             dma((n_tiles, 2)),
             dma((n_tiles - 2,)),
             dma((n_tiles - 2,)),
-            dma((2,)),
-            dma((2,)),
+            dma((2, 2)),
+            dma((2, 2)),
         ],
         compiler_params=pltpu.CompilerParams(
-            collective_id=0, has_side_effects=True, vmem_limit_bytes=62 * 1024 * 1024
+            collective_id=0, has_side_effects=True, vmem_limit_bytes=48 * 1024 * 1024
         ),
         cost_estimate=pl.CostEstimate(flops=8 * bins * n_time * channels**2, bytes_accessed=4 * block * bins * channels, transcendentals=0),
-    )(held_block, partner, spectra.reshape(2, n_time, bins, channels))
+    )(*(pltpu.with_memory_space_constraint(a, pltpu.HBM) for a in operands))
     return out[None, None]
 
 

time: 59.5 us -> 51.9 us (0.87)
  the two profiles are of different devices: /device:TPU:27 before, /device:TPU:24 now
where the time goes in v3:
time: 51.9 us; the launch traced here: 51.7 us
  Pallas kernels  50.9 us (98%)
  local copies, waits for them, and re-layouts  0.8 us (2%)
    pallas_call x1, Pallas kernels, per_device(): pl.pallas_call(functools.partial(kernel, n_pairs, n_x, weight), out_shape...  50.9 us

profile of v3, /device:TPU:24, one launch (start us, length us, event | category | flops | bytes accessed | tf_op | source)
XLA Modules:
  0.0 51.7 jit_solution(11384282940827623294)
XLA Ops:
  0.0 50.9 %shard_map.37 = f32[2,256,256]{2,1,0:T(8,128)S(1)} custom-call(s32[64]{0:T(128)} %held_hbm.1, s32[64]{0:T(128)} %partner_hbm.1, bf16[2,360,8,256]{3,2,1,0:T(8,128)(2,1)} %bitcast.3), custom_call_target="tpu_custom_call" | custom-call | flops 1509949440 | bytes 5898240 | tf_op jit(solution)/shard_map/pallas_call | solution.py:261
  50.9 0.8 %copy.5 = f32[1,1,2,256,256]{4,3,2,1,0:T(8,128)} copy(f32[1,1,2,256,256]{4,3,2,1,0:T(8,128)S(1)} %bitcast.2) | data formatting | bytes 1048576

commit v4 on v3

--- a/solution.py
+++ b/solution.py
@@ -18,7 +18,8 @@
 
 def kernel(
     n_pairs, n_x, weight, held_hbm, partner_hbm, x_ref, out_ref,
-    held_ref, partner_ref,    x_in, stage, grid_own, to_core, far, wide, tiles, parts, sent, sent_top, back, back_top, view,
+    held_ref, partner_ref, x_in, stage, grid_own, to_core, far, wide, tiles, parts,
+    sent, sent_top, back, back_top, view,
     in_sem, core_send, core_recv, z_send, z_recv, part_send, part_recv, back_send, back_recv,
 ):
     n_time = x_in.shape[1]
@@ -36,13 +37,14 @@
     has_to = p != n_pairs - 1 - last
 
     barrier = pltpu.get_barrier_semaphore()
+
+    @pl.when(has_from)
+    def _():
+        pl.semaphore_signal(barrier, inc=1, device_id=(z_from, d), device_id_type=MESH)
+
     peers = [(p, other)] + [(p, (x + k) % n_x * 2 + core) for k in range(1, n_x)]
     for peer in peers:
         pl.semaphore_signal(barrier, inc=1, device_id=peer, device_id_type=MESH)
-
-    @pl.when(has_from)
-    def _():
-        pl.semaphore_signal(barrier, inc=1, device_id=(z_from, d), device_id_type=MESH)
 
     chunks = in_sem.shape[0] - 2
     rows = n_time // chunks
@@ -56,21 +58,20 @@
         pltpu.make_async_copy(held_hbm, held_ref, in_sem.at[chunks]),
         pltpu.make_async_copy(partner_hbm, partner_ref, in_sem.at[chunks + 1]),
     ]
-    for load in loads + orders:
+    for load in loads:
         load.start()
 
     bins = 2 * n_x
 
     def owner(i):
         return (x + up * (1 + i) + n_x) % n_x
-
 
     def relayout(i, carry):
         t0 = pl.multiple_of(i * STEP, GROUP)
         for part in range(2):
             block = x_in[part, pl.ds(t0, STEP)].astype(jnp.float32).reshape(STEP * bins, 2 * LANES)
-            stage[part, 0] = block[:, :LANES]
-            stage[part, 1] = block[:, LANES:]
+            stage[part, 0, pl.ds(0, STEP * bins), :] = block[:, :LANES]
+            stage[part, 1, pl.ds(0, STEP * bins), :] = block[:, LANES:]
         r0 = pl.multiple_of(i * 2 * STEP, 16)
         for f in range(bins):
             for half in range(2):
@@ -147,6 +148,8 @@
                     device_id_type=MESH,
                 ).start()
 
+    for order in orders:
+        order.start()
     for i in range(n_x):
         core_copy(i).start()
     for i in range(n_x):
@@ -192,9 +195,9 @@
             tile = tiles[q]
             top = jnp.maximum(jnp.max(jnp.abs(tile), axis=0, keepdims=True), TINY)
             sent_top[half] = jnp.broadcast_to(top, sent_top.shape[1:])
+            back_copies(half)[0].start()
             sent[half] = jnp.round(tile * (LEVELS / top)).astype(jnp.int32).astype(jnp.int16)
-            for copy in back_copies(half):
-                copy.start()
+            back_copies(half)[1].start()
 
         return carry
 
@@ -271,7 +274,7 @@
             pltpu.SMEM((n_pairs,), jnp.int32),
             pltpu.SMEM((n_pairs,), jnp.int32),
             pltpu.VMEM((2, n_time, bins, channels), jnp.bfloat16),
-            pltpu.VMEM((2, 2, STEP * bins, LANES), jnp.float32),
+            pltpu.VMEM((2, 2, (STEP + 1) * bins, LANES), jnp.float32),
             pltpu.VMEM((bins, 2, block, LANES), jnp.bfloat16),
             pltpu.VMEM((n_x, 2, block, LANES), jnp.bfloat16),
             pltpu.VMEM((n_tiles, 2, block, LANES), jnp.bfloat16),
@@ -283,7 +286,7 @@
             pltpu.VMEM((2, LANES, 4 * LANES), jnp.int16),
             pltpu.VMEM((2, GROUP, 4 * LANES), jnp.float32),
             pltpu.VMEM((2, channels, channels), jnp.float32),
-            dma((5,)),
+            dma((7,)),
             dma((n_x,)),
             dma((n_x,)),
             dma((n_tiles, 2)),

time: 51.9 us -> 52.2 us (level)
  no operation moved by 1% of the time
where the time goes in v4:
time: 52.2 us; the launch traced here: 52.1 us
  Pallas kernels  51.2 us (98%)
  local copies, waits for them, and re-layouts  0.8 us (2%)
    pallas_call x1, Pallas kernels, per_device(): pl.pallas_call(functools.partial(kernel, n_pairs, n_x, weight), out_shape...  51.2 us

profile of v4, /device:TPU:24, one launch (start us, length us, event | category | flops | bytes accessed | tf_op | source)
XLA Modules:
  0.0 52.1 jit_solution(11998500339749299753)
XLA Ops:
  0.0 51.2 %shard_map.37 = f32[2,256,256]{2,1,0:T(8,128)S(1)} custom-call(s32[64]{0:T(128)} %held_hbm.1, s32[64]{0:T(128)} %partner_hbm.1, bf16[2,360,8,256]{3,2,1,0:T(8,128)(2,1)} %bitcast.3), custom_call_target="tpu_custom_call" | custom-call | flops 1509949440 | bytes 5898240 | tf_op jit(solution)/shard_map/pallas_call | solution.py:264
  51.3 0.8 %copy.5 = f32[1,1,2,256,256]{4,3,2,1,0:T(8,128)} copy(f32[1,1,2,256,256]{4,3,2,1,0:T(8,128)S(1)} %bitcast.2) | data formatting | bytes 1048576
